TPU v7x, 32 devices: a whole 2x2x4 slice. The times are simulated.
32 devices in a mesh: gx: 16 (over z, x, core), gy: 2 (over y).
Axes of the slice: x: 2, y: 2, z: 4, core: 2. Of those that a mesh axis runs over, the one named last changes fastest.
Arguments:
- potential: float32 [3, 1, 4096, 256], P(None, None, 'gx', 'gy'), may hold values from -8 to 8
- labels: int32 [1, 4096, 256], P(None, 'gx', 'gy'), may hold values from 0 to 7
- principal: float32 [2, 8], replicated, may hold values from 0.5 to 16
- off_diagonal: float32 [3, 8], replicated, may hold values from -0.4 to 0.4
Outputs:
- updated: float32 [3, 1, 4096, 256], P(None, None, 'gx', 'gy')
All inputs are finite; a program needn't handle non-finite values.
Results may differ from a plain program's by a relative error of at most 0.0017.
Values sent between devices are 32-bit elements; how exact they have to be, the bound alone decides.
A program may use at most 64 MiB of HBM per device.

v0:
```python
import functools

import jax
import jax.numpy as jnp
from jax import lax
from jax.experimental import pallas as pl
from jax.experimental.pallas import tpu as pltpu
from jax.sharding import PartitionSpec as P

MESH = pl.DeviceIdType.MESH
ROWS = 8


def sublane(shape):
    return lax.broadcasted_iota(jnp.int32, shape, len(shape) - 2)


def turn(x, by):
    size = x.shape[0]
    by = by % size
    return x if by == 0 else pltpu.roll(x, by, 0)


def following(q, last):
    wrap = turn(q[0], -1)
    wrap = jnp.where(sublane(wrap.shape) == 7, last, wrap)
    return wrap[None] if q.shape[0] == 1 else jnp.concatenate([q[1:], wrap[None]], 0)


def preceding(q):
    wrap = turn(q[-1], 1)
    first = jnp.where(sublane(wrap.shape) == 0, 0.0, wrap)[None]
    return (first if q.shape[0] == 1 else jnp.concatenate([first, q[:-1]], 0)), wrap


def split(q):
    pairs = q.reshape((q.shape[0] // 2, 2) + q.shape[1:])
    return pairs[:, 0], pairs[:, 1]


def merge(even, odd):
    return jnp.stack([even, odd], 1).reshape((2 * even.shape[0],) + even.shape[1:])


def wide(parts):
    return parts[0] if len(parts) == 1 else jnp.concatenate(parts, -1)


def strided(ref, steps):
    return jnp.stack([ref[pl.ds(t, 8, stride=steps), :] for t in range(steps)], 0)


def strided_wide(ref, steps):
    return wide([strided(ref.at[c], steps) for c in range(ref.shape[0])])


def put_wide(ref, value):
    for c in range(ref.shape[0]):
        ref[c] = value[:, c * 128 : (c + 1) * 128]


def lookup(tab, row, labels):
    out = jnp.broadcast_to(tab(row, 0), labels.shape)
    for phase in range(1, 8):
        out = jnp.where(labels == phase, jnp.broadcast_to(tab(row, phase), labels.shape), out)
    return out


def faces(k):
    nxt = following(k, k[0])
    e = 2.0 * k * nxt / (k + nxt)
    steps = k.shape[0]
    position = lax.broadcasted_iota(jnp.int32, k.shape, 0)
    return jnp.where((position == steps - 1) & (sublane(k.shape) == 7), 0.0, e)


def factor(e, damping):
    g = jnp.full(e.shape, damping, jnp.float32)
    levels = []
    g_end = jnp.zeros(e.shape[1:], jnp.float32)
    top = True
    while e.shape[0] > 1:
        e_even, e_odd = split(e)
        g_even, g_odd = split(g)
        r = 1.0 / (e_even + e_odd + g_odd)
        if top:
            is_end = (lax.broadcasted_iota(jnp.int32, r.shape, 0) == r.shape[0] - 1) & (sublane(r.shape) == 7)
            r = jnp.where(is_end, 0.0, r)
            right = jnp.where(is_end, 1.0, e_odd * r)
        else:
            right = e_odd * r
        left = e_even * r
        top = False
        levels.append((left, right, r))
        e = e_even * right
        moved, wrap = preceding(right * g_odd)
        g = g_even + left * g_odd + moved
        g_end = g_end + wrap
    e, g = e[0], g[0]
    sub = sublane(e.shape)
    for by in (1, 2, 4):
        chosen = sub % (2 * by) == by
        e_left = turn(e, by)
        r = jnp.where(chosen, 1.0 / (e_left + e + g), 0.0)
        left, right = e_left * r, e * r
        levels.append((left, right, r))
        e = e * turn(right, -by)
        wrap = turn(right * g, by)
        g = g + turn(left * g, -by) + jnp.where(sub == 0, 0.0, wrap)
        g_end = g_end + wrap
    return levels, e, g, g_end


def forward(levels, f):
    kept = []
    f_end = jnp.zeros(f.shape[1:], jnp.float32)
    for left, right, r in levels[:-3]:
        f_even, f_odd = split(f)
        kept.append(f_odd * r)
        moved, wrap = preceding(right * f_odd)
        f = f_even + left * f_odd + moved
        f_end = f_end + wrap
    f = f[0]
    sub = sublane(f.shape)
    for by, (left, right, r) in zip((1, 2, 4), levels[-3:]):
        kept.append(f * r)
        wrap = turn(right * f, by)
        f = f + turn(left * f, -by) + jnp.where(sub == 0, 0.0, wrap)
        f_end = f_end + wrap
    return kept, f, f_end


def backward(levels, kept, first, last):
    shape = kept[-1].shape
    sub = sublane(shape)
    v = jnp.broadcast_to(first, shape)
    last = jnp.broadcast_to(last, shape)
    for by, (left, right, r), own in zip((4, 2, 1), levels[:-4:-1], kept[:-4:-1]):
        after = jnp.where(sub >= 8 - by, last, turn(v, -by))
        v = jnp.where(sub % (2 * by) == by, own + left * turn(v, by) + right * after, v)
    v = v[None]
    for (left, right, r), own in zip(levels[:-3][::-1], kept[:-3][::-1]):
        odd = own + left * v + right * following(v, last)
        v = merge(v, odd)
    return v


def central(k):
    return 0.5 * (following(k, jnp.zeros_like(k[0])) - preceding(k)[0])


def put_record(box, me, rows):
    base = pl.multiple_of(me * len(rows), ROWS)
    rows = jnp.concatenate(rows, 0)
    for c in range(box.shape[0]):
        box[c, pl.ds(base, rows.shape[0]), :] = rows[:, c * 128 : (c + 1) * 128]


def matrix_rows(e, g, g_end, k, a):
    return [e[0:1], g[0:1], g_end[0:1], k[0, 0:1], k[-1, 7:8], a[0, 0:1], a[-1, 7:8], jnp.zeros_like(e[0:1])]


def forcing_rows(solved, b):
    return [s[1][0:1] for s in solved] + [s[2][0:1] for s in solved] + [b[0, 0:1], b[-1, 7:8]]


def copies(box, me, n, axis, send, recv):
    out = []
    rows = box.shape[1] // n
    for d in range(1, n):
        slot = box.at[:, pl.ds(pl.multiple_of(me * rows, ROWS), rows), :]
        out.append(
            pltpu.make_async_remote_copy(
                src_ref=slot,
                dst_ref=slot,
                send_sem=send.at[d],
                recv_sem=recv.at[d],
                device_id={axis: lax.rem(me + d, n)},
                device_id_type=MESH,
            )
        )
    return out


def get_row(box, n, q):
    parts = []
    rows = box.shape[1] // n
    for c in range(box.shape[0]):
        if n >= 8:
            parts.append(box[c, pl.ds(q, n, stride=rows), :])
            continue
        sub = sublane((8, 128)) % n
        out = jnp.broadcast_to(box[c, q : q + 1, :], (8, 128))
        for i in range(1, n):
            out = jnp.where(sub == i, box[c, i * rows + q : i * rows + q + 1, :], out)
        parts.append(out)
    return wide(parts)


def ring_factor(box, n):
    e, g, g_end, k_head, k_tail, a_head, a_tail = [get_row(box, n, q) for q in range(7)]
    k_next = turn(k_head, -1)
    link = 2.0 * k_tail * k_next / (k_tail + k_next)
    gain = [link, 0.5 * turn(a_head, -1)]
    loss = [turn(link, 1), turn(0.5 * a_tail, 1)]
    r = 1.0 / (e + link + g_end)
    left, right = e * r, link * r
    g = g + left * g_end + turn(right * g_end, 1)
    e = e * right
    levels = []
    by = 1
    while by < n:
        e_left = turn(e, by)
        s = 1.0 / (e_left + e + g)
        lo, hi = e_left * s, e * s
        levels.append((by, lo, hi))
        g = g + turn(lo * g, -by) + turn(hi * g, by)
        e = e * turn(hi, -by)
        by *= 2
    return gain, loss, r, left, right, levels, 1.0 / g


def ring_solve(box, n, skip, ring, order, me, first_out, last_out):
    gain, loss, r, left, right, levels, inv = ring
    f = [get_row(box, n, skip + q) for q in range(3)]
    f_end = [get_row(box, n, skip + q) for q in range(3, 6)]
    b_head, b_tail = get_row(box, n, skip + 6), get_row(box, n, skip + 7)
    gain = gain + [0.5 * turn(b_head, -1)]
    loss = loss + [turn(0.5 * b_tail, 1)]
    size = inv.shape[0]
    for i, which in enumerate(order):
        end = f_end[i] + gain[which]
        v = f[i] - loss[which] + left * end + turn(right * end, 1)
        for by, lo, hi in levels:
            v = v + turn(lo * v, -by) + turn(hi * v, by)
        v = v * inv
        first_out[i * size : (i + 1) * size, :] = v
        last_out[i * size : (i + 1) * size, :] = r * end + left * v + right * turn(v, -1)
    return [
        (first_out[pl.ds(i * size + me, 1), :], last_out[pl.ds(i * size + me, 1), :]) for i in range(3)
    ]


def kernel(nx, ny, damping, pot_hbm, lab_hbm, pri_hbm, off_hbm, out, pot, lab, pri, off, box_x, mat_y, box_y, labt, ft,
           first_x, last_x, first_y, last_y, send_x, recv_x, send_y, recv_y,
           send_my, recv_my, load):
    me_x, me_y = lax.axis_index("gx"), lax.axis_index("gy")
    barrier = pltpu.get_barrier_semaphore()
    for d in range(1, nx):
        pl.semaphore_signal(barrier, inc=1, device_id={"gx": lax.rem(me_x + d, nx)}, device_id_type=MESH)
    for d in range(1, ny):
        pl.semaphore_signal(barrier, inc=1, device_id={"gy": lax.rem(me_y + d, ny)}, device_id_type=MESH)

    loads = [
        pltpu.make_async_copy(src, dst, load.at[i])
        for i, (src, dst) in enumerate(((lab_hbm, lab), (pri_hbm, pri), (off_hbm, off), (pot_hbm, pot)))
    ]
    for copy in loads:
        copy.start()
    def tab(row, phase):
        ref, row = (pri, row) if row < 2 else (off, row - 2)
        return ref[row : row + 1, phase : phase + 1]

    rows, cols = lab.shape
    steps = rows // 8
    for copy in loads[:3]:
        copy.wait()
    labels = strided(lab, steps)
    k, a = lookup(tab, 0, labels), lookup(tab, 2, labels)
    e = faces(k)
    levels, e_in, g, g_end = factor(e, damping)
    b = lookup(tab, 3, labels)
    source = [e - preceding(e)[0], central(a), central(b)]
    loads[3].wait()
    solved = [forward(levels, damping * strided(pot.at[i], steps) + source[i]) for i in range(3)]
    put_record(box_x, me_x, matrix_rows(e_in, g, g_end, k, a) + forcing_rows(solved, b))
    pl.semaphore_wait(barrier, nx - 1 + ny - 1)
    sent_x = copies(box_x, me_x, nx, "gx", send_x, recv_x)
    for copy in sent_x:
        copy.start()

    lanes = labt.shape[0] * 128
    repeat = lanes // rows

    def across(q):
        flat = q.reshape(rows, cols)
        if repeat > 1:
            flat = jnp.concatenate([flat] * repeat, 0)
        return flat.T

    put_wide(labt, across(labels))
    ysteps = cols // 8
    labels_y = strided_wide(labt, ysteps)
    ky, ay, by = lookup(tab, 1, labels_y), lookup(tab, 2, labels_y), lookup(tab, 4, labels_y)
    ey = faces(ky)
    levels_y, ey_in, gy, gy_end = factor(ey, damping)
    put_record(mat_y, me_y, matrix_rows(ey_in, gy, gy_end, ky, ay))
    sent_my = copies(mat_y, me_y, ny, "gy", send_my, recv_my)
    for copy in sent_my:
        copy.start()
    source_y = [central(ay), ey - preceding(ey)[0], central(by)]

    for copy in sent_x:
        copy.wait_recv()
    ring_x = ring_factor(box_x, nx)
    ends = ring_solve(box_x, nx, ROWS, ring_x, (0, 1, 2), me_x, first_x, last_x)
    solved_y = []
    for i in range(3):
        half = backward(levels, solved[i][0], *ends[i])
        put_wide(ft.at[i], across(half))
        solved_y.append(forward(levels_y, damping * strided_wide(ft.at[i], ysteps) + source_y[i]))
    put_record(box_y, me_y, forcing_rows(solved_y, by))
    sent_y = copies(box_y, me_y, ny, "gy", send_y, recv_y)
    for copy in sent_y:
        copy.start()
    for copy in sent_my:
        copy.wait_recv()
    ring_y = ring_factor(mat_y, ny)
    for copy in sent_y:
        copy.wait_recv()
    ends = ring_solve(box_y, ny, 0, ring_y, (1, 0, 2), me_y, first_y, last_y)
    for i in range(3):
        v = backward(levels_y, solved_y[i][0], *ends[i])
        for t in range(ysteps):
            for c in range(lanes // 128):
                ft[i, c, pl.ds(t, 8, stride=ysteps), :] = v[t, :, c * 128 : (c + 1) * 128]
        back = jnp.concatenate([ft[i, c].T for c in range(lanes // 128)], 0)[:rows].reshape(steps, 8, cols)
        for t in range(steps):
            out[i, pl.ds(t, 8, stride=steps), :] = back[t]
    for copy in sent_x + sent_my + sent_y:
        copy.wait_send()


def local(potential, labels, principal, off_diagonal):
    nx, ny = lax.axis_size("gx"), lax.axis_size("gy")
    loads, _, rows, cols = potential.shape
    lanes = max(rows, 128)
    damping = 2.0 / (cols * cols)
    vmem = pl.BlockSpec(memory_space=pltpu.VMEM)
    hbm = pl.BlockSpec(memory_space=pltpu.HBM)
    result = pl.pallas_call(
        functools.partial(kernel, nx, ny, damping),
        out_shape=jax.ShapeDtypeStruct((loads, rows, cols), jnp.float32),
        in_specs=[hbm] * 4,
        out_specs=vmem,
        scratch_shapes=[
            pltpu.VMEM((loads, rows, cols), jnp.float32),
            pltpu.VMEM((rows, cols), jnp.int32),
            pltpu.VMEM(principal.shape, jnp.float32),
            pltpu.VMEM(off_diagonal.shape, jnp.float32),
            pltpu.VMEM((1, nx * 2 * ROWS, cols), jnp.float32),
            pltpu.VMEM((lanes // 128, ny * ROWS, 128), jnp.float32),
            pltpu.VMEM((lanes // 128, ny * ROWS, 128), jnp.float32),
            pltpu.VMEM((lanes // 128, cols, 128), jnp.int32),
            pltpu.VMEM((loads, lanes // 128, cols, 128), jnp.float32),
            pltpu.VMEM((loads * max(nx, 8), cols), jnp.float32),
            pltpu.VMEM((loads * max(nx, 8), cols), jnp.float32),
            pltpu.VMEM((loads * max(ny, 8), lanes), jnp.float32),
            pltpu.VMEM((loads * max(ny, 8), lanes), jnp.float32),
            pltpu.SemaphoreType.DMA((nx,)),
            pltpu.SemaphoreType.DMA((nx,)),
            pltpu.SemaphoreType.DMA((ny,)),
            pltpu.SemaphoreType.DMA((ny,)),
            pltpu.SemaphoreType.DMA((ny,)),
            pltpu.SemaphoreType.DMA((ny,)),
            pltpu.SemaphoreType.DMA((4,)),
        ],
        compiler_params=pltpu.CompilerParams(
            collective_id=0, has_side_effects=True, vmem_limit_bytes=32 * 1024 * 1024
        ),
    )(potential.reshape(loads, rows, cols), labels.reshape(rows, cols), principal, off_diagonal)
    return result.reshape(potential.shape)


def solution(mesh):
    in_specs = (P(None, None, "gx", "gy"), P(None, "gx", "gy"), P(), P())
    out_specs = P(None, None, "gx", "gy")
    return jax.shard_map(local, mesh=mesh, in_specs=in_specs, out_specs=out_specs, check_vma=False)
```

profile of v0, /device:TPU:0, one launch (start us, length us, event | category | flops | bytes accessed | tf_op | source)
XLA Modules:
  0.0 16.7 jit_solution(6182928685543763620)
XLA Ops:
  0.0 0.0 copy-start.2
  0.0 0.0 copy-start.3
  0.0 0.7 %copy-done.2 = f32[3,8]{1,0:T(4,128)S(1)} copy-done((f32[3,8]{1,0:T(4,128)S(1)}, f32[3,8]{1,0:T(4,128)}, u32[]{:S(2)}) %copy-start.2) | copy-done | bytes 120
  0.7 0.0 copy-done.3
  0.7 0.0 copy-start
  0.7 1.0 %copy-done = f32[3,1,256,128]{3,2,1,0:T(8,128)S(1)} copy-done((f32[3,1,256,128]{3,2,1,0:T(8,128)S(1)}, f32[3,1,256,128]{3,2,1,0:T(8,128)}, u32[]{:S(2)}) %copy-start) | copy-done | bytes 393240
  1.7 0.0 copy-start.1
  1.7 0.9 %copy-done.1 = s32[1,256,128]{2,1,0:T(8,128)S(1)} copy-done((s32[1,256,128]{2,1,0:T(8,128)S(1)}, s32[1,256,128]{2,1,0:T(8,128)}, u32[]{:S(2)}) %copy-start.1) | copy-done | bytes 131096
  2.6 13.3 %shard_map.46 = f32[3,256,128]{2,1,0:T(8,128)S(1)} custom-call(f32[3,256,128]{2,1,0:T(8,128)S(1)} %bitcast.6, s32[256,128]{1,0:T(8,128)S(1)} %bitcast.7, f32[2,8]{1,0:T(2,128)S(1)} %copy-done.3, f32[3,8]{1,0:T(4,128)S(1)} %copy-done.2), custom_call_target="tpu_custom_call" | custom-call | tf_op jit(solution)/shard_map/pallas_call | solution.py:341
  15.9 0.7 %copy.7 = f32[3,1,256,128]{3,2,1,0:T(8,128)} copy(f32[3,1,256,128]{3,2,1,0:T(8,128)S(1)} %bitcast.5) | data formatting | bytes 786432
Async XLA Ops:
  0.0 0.7 %copy-start.2 = (f32[3,8]{1,0:T(4,128)S(1)}, f32[3,8]{1,0:T(4,128)}, u32[]{:S(2)}) copy-start(f32[3,8]{1,0:T(4,128)} %off_hbm.1) | copy-start | bytes 292
  0.0 0.7 %copy-start.3 = (f32[2,8]{1,0:T(2,128)S(1)}, f32[2,8]{1,0:T(2,128)}, u32[]{:S(2)}) copy-start(f32[2,8]{1,0:T(2,128)} %pri_hbm.1) | copy-start | bytes 196
  0.7 1.0 %copy-start = (f32[3,1,256,128]{3,2,1,0:T(8,128)S(1)}, f32[3,1,256,128]{3,2,1,0:T(8,128)}, u32[]{:S(2)}) copy-start(f32[3,1,256,128]{3,2,1,0:T(8,128)} %param.4) | copy-start | bytes 1179652
  1.7 0.9 %copy-start.1 = (s32[1,256,128]{2,1,0:T(8,128)S(1)}, s32[1,256,128]{2,1,0:T(8,128)}, u32[]{:S(2)}) copy-start(s32[1,256,128]{2,1,0:T(8,128)} %param.5) | copy-start | bytes 393220
where the time goes:
time: 16.9 us; the launch traced here: 16.7 us
  Pallas kernels  13.3 us (79%)
  local copies, waits for them, and re-layouts  3.34 us (20%)
    pallas_call x1, Pallas kernels, local(): pl.pallas_call(functools.partial(kernel, nx, ny, damping), out_shape=jax....  13.3 us
    unnamed x9, local copies, waits for them, and re-layouts  3.34 us

commit v1 on v0

--- a/solution.py
+++ b/solution.py
@@ -340,7 +340,7 @@
     hbm = pl.BlockSpec(memory_space=pltpu.HBM)
     result = pl.pallas_call(
         functools.partial(kernel, nx, ny, damping),
-        out_shape=jax.ShapeDtypeStruct((loads, rows, cols), jnp.float32),
+        out_shape=pltpu.VMEM((loads, rows, cols), jnp.float32),
         in_specs=[hbm] * 4,
         out_specs=vmem,
         scratch_shapes=[
@@ -368,7 +368,7 @@
         compiler_params=pltpu.CompilerParams(
             collective_id=0, has_side_effects=True, vmem_limit_bytes=32 * 1024 * 1024
         ),
-    )(potential.reshape(loads, rows, cols), labels.reshape(rows, cols), principal, off_diagonal)
+    )(*[pltpu.with_memory_space_constraint(x, pltpu.HBM) for x in (potential.reshape(loads, rows, cols), labels.reshape(rows, cols), principal, off_diagonal)])
     return result.reshape(potential.shape)
 
 

time: 16.9 us -> 14.7 us (0.87)
  local copies, waits for them, and re-layouts: 3.34 us -> 0.75 us
  Pallas kernels: 13.3 us -> 13.8 us
    unnamed x9 -> x1, local copies, waits for them, and re-layouts: 3.34 us -> 0.75 us
    pallas_call x1, Pallas kernels: 13.3 us -> 13.8 us  [local(): pl.pallas_call(functools.partial(kernel, nx, ny, damping), out_shape=pltp...]
where the time goes in v1:
time: 14.7 us; the launch traced here: 14.6 us
  Pallas kernels  13.8 us (94%)
  local copies, waits for them, and re-layouts  0.75 us (5%)
    pallas_call x1, Pallas kernels, local(): pl.pallas_call(functools.partial(kernel, nx, ny, damping), out_shape=pltp...  13.8 us
    unnamed x1, local copies, waits for them, and re-layouts  0.75 us

profile of v1, /device:TPU:0, one launch (start us, length us, event | category | flops | bytes accessed | tf_op | source)
XLA Modules:
  0.0 14.6 jit_solution(8468089465123507900)
XLA Ops:
  0.0 13.8 %shard_map.46 = f32[3,256,128]{2,1,0:T(8,128)S(1)} custom-call(f32[3,256,128]{2,1,0:T(8,128)} %bitcast.6, s32[256,128]{1,0:T(8,128)} %bitcast.7, f32[2,8]{1,0:T(2,128)} %pri_hbm.1, f32[3,8]{1,0:T(4,128)} %off_hbm.1), custom_call_target="tpu_custom_call" | custom-call | tf_op jit(solution)/shard_map/pallas_call | solution.py:341
  13.8 0.7 %copy.7 = f32[3,1,256,128]{3,2,1,0:T(8,128)} copy(f32[3,1,256,128]{3,2,1,0:T(8,128)S(1)} %bitcast.5) | data formatting | bytes 786432

commit v2 on v1

v2 whole, which is shorter than its diff:
```python
import functools

import jax
import jax.numpy as jnp
from jax import lax
from jax.experimental import pallas as pl
from jax.experimental.pallas import tpu as pltpu
from jax.sharding import PartitionSpec as P

MESH = pl.DeviceIdType.MESH
ROWS = 8


def sublane(shape):
    return lax.broadcasted_iota(jnp.int32, shape, len(shape) - 2)


def turn(x, by):
    size = x.shape[0]
    by = by % size
    return x if by == 0 else pltpu.roll(x, by, 0)


def following(q, last):
    wrap = turn(q[0], -1)
    wrap = jnp.where(sublane(wrap.shape) == 7, last, wrap)
    return wrap[None] if q.shape[0] == 1 else jnp.concatenate([q[1:], wrap[None]], 0)


def preceding(q):
    wrap = turn(q[-1], 1)
    first = jnp.where(sublane(wrap.shape) == 0, 0.0, wrap)[None]
    return (first if q.shape[0] == 1 else jnp.concatenate([first, q[:-1]], 0)), wrap


def split(q):
    pairs = q.reshape((q.shape[0] // 2, 2) + q.shape[1:])
    return pairs[:, 0], pairs[:, 1]


def merge(even, odd):
    return jnp.stack([even, odd], 1).reshape((2 * even.shape[0],) + even.shape[1:])


def wide(parts):
    return parts[0] if len(parts) == 1 else jnp.concatenate(parts, -1)


def strided(ref, steps):
    return jnp.stack([ref[pl.ds(t, 8, stride=steps), :] for t in range(steps)], 0)


def strided_wide(ref, steps):
    return wide([strided(ref.at[c], steps) for c in range(ref.shape[0])])


def put_wide(ref, value):
    for c in range(ref.shape[0]):
        ref[c] = value[:, c * 128 : (c + 1) * 128]


def get_wide(ref):
    return wide([ref[c] for c in range(ref.shape[0])])


def spread(ref, row):
    lane = lax.broadcasted_iota(jnp.int32, (8, 128), 1)
    out = jnp.broadcast_to(ref[row : row + 1, 0:1], (8, 128))
    for phase in range(1, 8):
        out = jnp.where(lane == phase, jnp.broadcast_to(ref[row : row + 1, phase : phase + 1], (8, 128)), out)
    return out


def lookup(table, labels):
    width = labels.shape[-1]
    flat = labels.reshape(-1, 8, width)
    out = []
    for t in range(flat.shape[0]):
        parts = [
            jnp.take_along_axis(table, flat[t, :, c : c + 128], axis=1, mode="promise_in_bounds")
            for c in range(0, width, 128)
        ]
        out.append(wide(parts))
    return jnp.stack(out, 0).reshape(labels.shape)


def faces(half_inverse):
    e = 1.0 / (half_inverse + following(half_inverse, half_inverse[0]))
    position = lax.broadcasted_iota(jnp.int32, e.shape, 0)
    return jnp.where((position == e.shape[0] - 1) & (sublane(e.shape) == 7), 0.0, e)


def factor(e, damping):
    g = jnp.full(e.shape, damping, jnp.float32)
    levels = []
    g_end = jnp.zeros(e.shape[1:], jnp.float32)
    top = True
    while e.shape[0] > 1:
        e_even, e_odd = split(e)
        g_even, g_odd = split(g)
        r = 1.0 / (e_even + e_odd + g_odd)
        if top:
            is_end = (lax.broadcasted_iota(jnp.int32, r.shape, 0) == r.shape[0] - 1) & (sublane(r.shape) == 7)
            r = jnp.where(is_end, 0.0, r)
            right = jnp.where(is_end, 1.0, e_odd * r)
        else:
            right = e_odd * r
        left = e_even * r
        top = False
        levels.append((left, right, r))
        e = e_even * right
        moved, wrap = preceding(right * g_odd)
        g = g_even + left * g_odd + moved
        g_end = g_end + wrap
    e, g = e[0], g[0]
    sub = sublane(e.shape)
    for by in (1, 2, 4):
        chosen = sub % (2 * by) == by
        e_left = turn(e, by)
        r = jnp.where(chosen, 1.0 / (e_left + e + g), 0.0)
        left, right = e_left * r, e * r
        levels.append((left, right, r))
        e = e * turn(right, -by)
        wrap = turn(right * g, by)
        g = g + turn(left * g, -by) + jnp.where(sub == 0, 0.0, wrap)
        g_end = g_end + wrap
    return levels, e, g, g_end


def forward(levels, f):
    kept = []
    f_end = jnp.zeros(f.shape[1:], jnp.float32)
    for left, right, r in levels[:-3]:
        f_even, f_odd = split(f)
        kept.append(f_odd * r)
        moved, wrap = preceding(right * f_odd)
        f = f_even + left * f_odd + moved
        f_end = f_end + wrap
    f = f[0]
    sub = sublane(f.shape)
    for by, (left, right, r) in zip((1, 2, 4), levels[-3:]):
        kept.append(f * r)
        wrap = turn(right * f, by)
        f = f + turn(left * f, -by) + jnp.where(sub == 0, 0.0, wrap)
        f_end = f_end + wrap
    return kept, f, f_end


def backward(levels, kept, first, last):
    shape = kept[-1].shape
    sub = sublane(shape)
    v = jnp.broadcast_to(first, shape)
    last = jnp.broadcast_to(last, shape)
    for by, (left, right, r), own in zip((4, 2, 1), levels[:-4:-1], kept[:-4:-1]):
        after = jnp.where(sub >= 8 - by, last, turn(v, -by))
        v = jnp.where(sub % (2 * by) == by, own + left * turn(v, by) + right * after, v)
    v = v[None]
    for (left, right, r), own in zip(levels[:-3][::-1], kept[:-3][::-1]):
        odd = own + left * v + right * following(v, last)
        v = merge(v, odd)
    return v


def homogeneous(levels):
    none = [jnp.zeros_like(r) for _, _, r in levels]
    row = jnp.zeros_like(levels[-1][2][0:1])
    return backward(levels, none, row + 1.0, row), backward(levels, none, row, row + 1.0)


def central(k):
    return 0.5 * (following(k, jnp.zeros_like(k[0])) - preceding(k)[0])


def put_record(box, me, rows):
    for q, row in enumerate(rows):
        box[q, pl.ds(me, 1), :] = row


def partner(me, mask, n):
    if n & (n - 1):
        return lax.rem(me + mask, n)
    out = me
    bit = 1
    while bit < n:
        if mask & bit:
            out = out + bit * (1 - 2 * lax.rem(lax.div(me, bit), 2))
        bit *= 2
    return out


def send_all(box, me, n, axis, send, recv):
    slot = box.at[:, pl.ds(me, 1), :]
    for mask in range(n - 1, 0, -1):
        pltpu.make_async_remote_copy(
            src_ref=slot,
            dst_ref=slot,
            send_sem=send,
            recv_sem=recv,
            device_id={axis: partner(me, mask, n)},
            device_id_type=MESH,
        ).start()


def wait_all(box, n, sem):
    rest = box.at[:, pl.ds(0, n - 1), :]
    pltpu.make_async_copy(rest, rest, sem).wait()


def get_row(box, n, q):
    if n >= 8:
        return box[q]
    width = box.shape[-1]
    sub = sublane((8, width)) % n
    out = jnp.broadcast_to(box[q, 0:1, :], (8, width))
    for i in range(1, n):
        out = jnp.where(sub == i, jnp.broadcast_to(box[q, i : i + 1, :], (8, width)), out)
    return out


def ring_factor(box, n, tables):
    e, g, g_end, head, tail = [get_row(box, n, q) for q in range(5)]
    head, tail = head.astype(jnp.int32), tail.astype(jnp.int32)
    k_table, a_table, b_table = tables
    link = 1.0 / (lookup(k_table, tail) + turn(lookup(k_table, head), -1))
    gain = [link, 0.5 * turn(lookup(a_table, head), -1), 0.5 * turn(lookup(b_table, head), -1)]
    loss = [turn(link, 1), turn(0.5 * lookup(a_table, tail), 1), turn(0.5 * lookup(b_table, tail), 1)]
    r = 1.0 / (e + link + g_end)
    left, right = e * r, link * r
    g = g + left * g_end + turn(right * g_end, 1)
    e = e * right
    levels = []
    by = 1
    while by < n:
        e_left = turn(e, by)
        s = 1.0 / (e_left + e + g)
        lo, hi = e_left * s, e * s
        levels.append((by, lo, hi))
        g = g + turn(lo * g, -by) + turn(hi * g, by)
        e = e * turn(hi, -by)
        by *= 2
    return gain, loss, r, left, right, levels, 1.0 / g


def ring_solve(box, n, ring, order, me, first_out, last_out):
    gain, loss, r, left, right, levels, inv = ring
    size = inv.shape[0]
    for i, which in enumerate(order):
        end = get_row(box, n, 3 + i) + gain[which]
        v = get_row(box, n, i) - loss[which] + left * end + turn(right * end, 1)
        for by, lo, hi in levels:
            v = v + turn(lo * v, -by) + turn(hi * v, by)
        v = v * inv
        first_out[i * size : (i + 1) * size, :] = v
        last_out[i * size : (i + 1) * size, :] = r * end + left * v + right * turn(v, -1)
    return [
        (first_out[pl.ds(i * size + me, 1), :], last_out[pl.ds(i * size + me, 1), :]) for i in range(3)
    ]


def total(x):
    x = jnp.sum(x, axis=0) if x.ndim == 3 else x
    for by in (1, 2, 4):
        x = x + turn(x, by)
    return x[0:1]


def kernel(nx, ny, damping, pot_hbm, lab_hbm, pri_hbm, off_hbm, out, pot, lab, pri, off, mat_x, box_x, mat_y, box_y,
           labt, ft, ends_y, first_x, last_x, first_y, last_y, send_x, recv_x, send_y, recv_y, load):
    me_x, me_y = lax.axis_index("gx"), lax.axis_index("gy")
    loads, steps, _, cols = pot.shape
    rows = steps * 8
    for s in range(8):
        pltpu.make_async_copy(lab_hbm.at[pl.ds(s * steps, steps), :], lab.at[:, s, :], load.at[0]).start()
    small = [pltpu.make_async_copy(src, dst, load.at[i]) for i, (src, dst) in enumerate(((pri_hbm, pri), (off_hbm, off)), 1)]
    for copy in small:
        copy.start()
    barrier = pltpu.get_barrier_semaphore()
    for mask in range(1, nx):
        pl.semaphore_signal(barrier, inc=1, device_id={"gx": partner(me_x, mask, nx)}, device_id_type=MESH)
    for mask in range(1, ny):
        pl.semaphore_signal(barrier, inc=1, device_id={"gy": partner(me_y, mask, ny)}, device_id_type=MESH)
    for s in range(8):
        pltpu.make_async_copy(pot_hbm.at[:, pl.ds(s * steps, steps), :], pot.at[:, :, s, :], load.at[3]).start()

    for copy in small:
        copy.wait()
    kx_table, ky_table = 0.5 / spread(pri, 0), 0.5 / spread(pri, 1)
    xy_table, xz_table, yz_table = [spread(off, row) for row in range(3)]
    pltpu.make_async_copy(lab, lab, load.at[0]).wait()
    labels = lab[...]
    e = faces(lookup(kx_table, labels))
    levels, e_in, g, g_end = factor(e, damping)
    head, tail = labels[0, 0:1].astype(jnp.float32), labels[-1, 7:8].astype(jnp.float32)
    put_record(mat_x, me_x, [e_in[0:1], g[0:1], g_end[0:1], head, tail])
    pl.semaphore_wait(barrier, nx - 1 + ny - 1)
    send_all(mat_x, me_x, nx, "gx", send_x.at[0], recv_x.at[0])
    a, b = lookup(xy_table, labels), lookup(xz_table, labels)
    source = [e - preceding(e)[0], central(a), central(b)]
    pltpu.make_async_copy(pot, pot, load.at[3]).wait()
    solved = [forward(levels, damping * pot[i] + source[i]) for i in range(3)]
    put_record(box_x, me_x, [s[1][0:1] for s in solved] + [s[2][0:1] for s in solved])
    send_all(box_x, me_x, nx, "gx", send_x.at[1], recv_x.at[1])

    lanes = labt.shape[0] * 128
    repeat = lanes // rows

    def across(q):
        flat = q.reshape(rows, cols)
        if repeat > 1:
            flat = jnp.concatenate([flat] * repeat, 0)
        return flat.T

    def along(q, slot):
        for t in range(ysteps):
            for c in range(lanes // 128):
                ft[slot, c, pl.ds(t, 8, stride=ysteps), :] = q[t, :, c * 128 : (c + 1) * 128]
        natural = get_wide(ft.at[slot])
        return natural, natural.T[:rows].reshape(steps, 8, cols)

    put_wide(labt, across(labels))
    ysteps = cols // 8
    labels_y = strided_wide(labt, ysteps)
    ey = faces(lookup(ky_table, labels_y))
    levels_y, ey_in, gy, gy_end = factor(ey, damping)
    head_y, tail_y = labels_y[0, 0:1].astype(jnp.float32), labels_y[-1, 7:8].astype(jnp.float32)
    put_record(mat_y, me_y, [ey_in[0:1], gy[0:1], gy_end[0:1], head_y, tail_y])
    send_all(mat_y, me_y, ny, "gy", send_y.at[0], recv_y.at[0])
    ay, by = lookup(xy_table, labels_y), lookup(yz_table, labels_y)
    source_y = [central(ay), ey - preceding(ey)[0], central(by)]
    base_y = [forward(levels_y, q) for q in source_y]
    zero = jnp.zeros((1, cols), jnp.float32)
    inner = [backward(levels, kept, zero, zero) for kept, _, _ in solved]
    first_part, last_part = homogeneous(levels)
    first_y_part, last_y_part = homogeneous(levels_y)
    first_weight, first_share = along(first_y_part, 0)
    last_weight, last_share = along(last_y_part, 1)
    first_weight, last_weight = damping * first_weight, damping * last_weight

    wait_all(mat_y, ny, recv_y.at[0])
    ring_y = ring_factor(mat_y, ny, (ky_table, xy_table, yz_table))
    wait_all(mat_x, nx, recv_x.at[0])
    ring_x = ring_factor(mat_x, nx, (kx_table, xy_table, xz_table))
    wait_all(box_x, nx, recv_x.at[1])
    ends = ring_solve(box_x, nx, ring_x, (0, 1, 2), me_x, first_x, last_x)
    turned = [across(inner[i] + first_part * ends[i][0] + last_part * ends[i][1]) for i in range(3)]
    firsts = [base_y[i][1][0:1] + total((first_weight * turned[i]).reshape(ysteps, 8, lanes)) for i in range(3)]
    lasts = [base_y[i][2][0:1] + total((last_weight * turned[i]).reshape(ysteps, 8, lanes)) for i in range(3)]
    put_record(box_y, me_y, firsts + lasts)
    send_all(box_y, me_y, ny, "gy", send_y.at[1], recv_y.at[1])

    row = jnp.zeros((1, lanes), jnp.float32)
    own = []
    for i in range(3):
        put_wide(ft.at[2 + i], turned[i])
        kept = forward(levels_y, damping * strided_wide(ft.at[2 + i], ysteps) + source_y[i])[0]
        own.append(along(backward(levels_y, kept, row, row), 2 + i)[1])
    wait_all(box_y, ny, recv_y.at[1])
    ends = ring_solve(box_y, ny, ring_y, (1, 0, 2), me_y, first_y, last_y)
    for i in range(3):
        ends_y[2 * i : 2 * i + 1, :] = ends[i][0]
        ends_y[2 * i + 1 : 2 * i + 2, :] = ends[i][1]
    column = jnp.concatenate([ends_y[...]] * 16, 0).T[:rows].reshape(steps, 8, 128)
    for i in range(3):
        for t in range(steps):
            out[i, t] = (own[i][t] + first_share[t] * column[t, :, 2 * i : 2 * i + 1]
                         + last_share[t] * column[t, :, 2 * i + 1 : 2 * i + 2])
    for box, n, sem in ((mat_x, nx, send_x.at[0]), (box_x, nx, send_x.at[1]), (mat_y, ny, send_y.at[0]), (box_y, ny, send_y.at[1])):
        wait_all(box, n, sem)


def store(v, out, sem):
    steps = v.shape[1]
    for s in range(8):
        pltpu.make_async_copy(v.at[:, :, s, :], out.at[:, pl.ds(s * steps, steps), :], sem).start()
    pltpu.make_async_copy(v, v, sem).wait()


def local(potential, labels, principal, off_diagonal):
    nx, ny = lax.axis_size("gx"), lax.axis_size("gy")
    loads, _, rows, cols = potential.shape
    lanes = max(rows, 128)
    steps = rows // 8
    damping = 2.0 / (cols * cols)
    vmem = pl.BlockSpec(memory_space=pltpu.VMEM)
    hbm = pl.BlockSpec(memory_space=pltpu.HBM)
    args = (potential.reshape(loads, rows, cols), labels.reshape(rows, cols), principal, off_diagonal)
    result = pl.pallas_call(
        functools.partial(kernel, nx, ny, damping),
        out_shape=pltpu.VMEM((loads, steps, 8, cols), jnp.float32),
        in_specs=[hbm] * 4,
        out_specs=vmem,
        scratch_shapes=[
            pltpu.VMEM((loads, steps, 8, cols), jnp.float32),
            pltpu.VMEM((steps, 8, cols), jnp.int32),
            pltpu.VMEM(principal.shape, jnp.float32),
            pltpu.VMEM(off_diagonal.shape, jnp.float32),
            pltpu.VMEM((5, nx, cols), jnp.float32),
            pltpu.VMEM((6, nx, cols), jnp.float32),
            pltpu.VMEM((5, ny, lanes), jnp.float32),
            pltpu.VMEM((6, ny, lanes), jnp.float32),
            pltpu.VMEM((lanes // 128, cols, 128), jnp.int32),
            pltpu.VMEM((5, lanes // 128, cols, 128), jnp.float32),
            pltpu.VMEM((8, lanes), jnp.float32),
            pltpu.VMEM((loads * max(nx, 8), cols), jnp.float32),
            pltpu.VMEM((loads * max(nx, 8), cols), jnp.float32),
            pltpu.VMEM((loads * max(ny, 8), lanes), jnp.float32),
            pltpu.VMEM((loads * max(ny, 8), lanes), jnp.float32),
            pltpu.SemaphoreType.DMA((2,)),
            pltpu.SemaphoreType.DMA((2,)),
            pltpu.SemaphoreType.DMA((2,)),
            pltpu.SemaphoreType.DMA((2,)),
            pltpu.SemaphoreType.DMA((4,)),
        ],
        compiler_params=pltpu.CompilerParams(
            collective_id=0, has_side_effects=True, vmem_limit_bytes=32 * 1024 * 1024
        ),
    )(*[pltpu.with_memory_space_constraint(x, pltpu.HBM) for x in args])
    result = pl.pallas_call(
        store,
        out_shape=pltpu.HBM((loads, rows, cols), jnp.float32),
        in_specs=[vmem],
        out_specs=hbm,
        scratch_shapes=[pltpu.SemaphoreType.DMA],
        compiler_params=pltpu.CompilerParams(vmem_limit_bytes=8 * 1024 * 1024),
    )(pltpu.with_memory_space_constraint(result, pltpu.VMEM))
    return result.reshape(potential.shape)


def solution(mesh):
    in_specs = (P(None, None, "gx", "gy"), P(None, "gx", "gy"), P(), P())
    out_specs = P(None, None, "gx", "gy")
    return jax.shard_map(local, mesh=mesh, in_specs=in_specs, out_specs=out_specs, check_vma=False)
```

time: 14.7 us -> 14.5 us (0.986)
  local copies, waits for them, and re-layouts: 0.75 us -> 0 us
  Pallas kernels: 13.8 us -> 14.3 us
    unnamed x1 -> x0, local copies, waits for them, and re-layouts: 0.75 us -> none
    pallas_call x0 -> x1, Pallas kernels: none -> 0.74 us  [local(): pl.pallas_call(store, out_shape=pltpu.HBM((loads, rows, cols), jnp.float3...]
    pallas_call x1, Pallas kernels: 13.8 us -> 13.5 us  [local(): pl.pallas_call(functools.partial(kernel, nx, ny, damping), out_shape=pltp...]
where the time goes in v2:
time: 14.5 us; the launch traced here: 14.3 us
  Pallas kernels  14.3 us (99%)
    pallas_call x1, Pallas kernels, local(): pl.pallas_call(functools.partial(kernel, nx, ny, damping), out_shape=pltp...  13.5 us
    pallas_call x1, Pallas kernels, local(): pl.pallas_call(store, out_shape=pltpu.HBM((loads, rows, cols), jnp.float3...  0.74 us

profile of v2, /device:TPU:0, one launch (start us, length us, event | category | flops | bytes accessed | tf_op | source)
XLA Modules:
  0.0 14.3 jit_solution(17549492831615950489)
XLA Ops:
  0.0 13.5 %shard_map.46.v = f32[3,32,8,128]{3,2,1,0:T(8,128)S(1)} custom-call(f32[3,256,128]{2,1,0:T(8,128)} %bitcast.5, s32[256,128]{1,0:T(8,128)} %bitcast.6, f32[2,8]{1,0:T(2,128)} %pri_hbm.1, f32[3,8]{1,0:T(4,128)} %off_hbm.1), custom_call_target="tpu_custom_call" | custom-call | tf_op jit(solution)/shard_map/pallas_call | solution.py:387
  13.5 0.7 %shard_map.47 = f32[3,256,128]{2,1,0:T(8,128)} custom-call(f32[3,32,8,128]{3,2,1,0:T(8,128)S(1)} %shard_map.46.v), custom_call_target="tpu_custom_call" | custom-call | tf_op jit(solution)/shard_map/pallas_call | solution.py:418

commit v3 on v2

--- a/solution.py
+++ b/solution.py
@@ -171,6 +171,10 @@
     return 0.5 * (following(k, jnp.zeros_like(k[0])) - preceding(k)[0])
 
 
+def matrix_rows(e, g, g_end, k, a, b):
+    return [e[0:1], g[0:1], g_end[0:1]] + [q for x in (k, a, b) for q in (x[0, 0:1], x[-1, 7:8])]
+
+
 def put_record(box, me, rows):
     for q, row in enumerate(rows):
         box[q, pl.ds(me, 1), :] = row
@@ -190,13 +194,13 @@
 
 def send_all(box, me, n, axis, send, recv):
     slot = box.at[:, pl.ds(me, 1), :]
-    for mask in range(n - 1, 0, -1):
+    for k in range(n - 1):
         pltpu.make_async_remote_copy(
             src_ref=slot,
             dst_ref=slot,
             send_sem=send,
             recv_sem=recv,
-            device_id={axis: partner(me, mask, n)},
+            device_id={axis: k + lax.div(k - me + n, n)},
             device_id_type=MESH,
         ).start()
 
@@ -217,13 +221,11 @@
     return out
 
 
-def ring_factor(box, n, tables):
-    e, g, g_end, head, tail = [get_row(box, n, q) for q in range(5)]
-    head, tail = head.astype(jnp.int32), tail.astype(jnp.int32)
-    k_table, a_table, b_table = tables
-    link = 1.0 / (lookup(k_table, tail) + turn(lookup(k_table, head), -1))
-    gain = [link, 0.5 * turn(lookup(a_table, head), -1), 0.5 * turn(lookup(b_table, head), -1)]
-    loss = [turn(link, 1), turn(0.5 * lookup(a_table, tail), 1), turn(0.5 * lookup(b_table, tail), 1)]
+def ring_factor(box, n):
+    e, g, g_end, k_head, k_tail, a_head, a_tail, b_head, b_tail = [get_row(box, n, q) for q in range(9)]
+    link = 1.0 / (k_tail + turn(k_head, -1))
+    gain = [link, 0.5 * turn(a_head, -1), 0.5 * turn(b_head, -1)]
+    loss = [turn(link, 1), turn(0.5 * a_tail, 1), turn(0.5 * b_tail, 1)]
     r = 1.0 / (e + link + g_end)
     left, right = e * r, link * r
     g = g + left * g_end + turn(right * g_end, 1)
@@ -264,8 +266,8 @@
     return x[0:1]
 
 
-def kernel(nx, ny, damping, pot_hbm, lab_hbm, pri_hbm, off_hbm, out, pot, lab, pri, off, mat_x, box_x, mat_y, box_y,
-           labt, ft, ends_y, first_x, last_x, first_y, last_y, send_x, recv_x, send_y, recv_y, load):
+def kernel(nx, ny, damping, pot_hbm, lab_hbm, pri_hbm, off_hbm, own_out, first_out, last_out, ends_out, pot, lab, pri, off, box_x, mat_y, box_y,
+           labt, ft, first_x, last_x, first_y, last_y, send_x, recv_x, send_y, recv_y, load):
     me_x, me_y = lax.axis_index("gx"), lax.axis_index("gy")
     loads, steps, _, cols = pot.shape
     rows = steps * 8
@@ -288,17 +290,15 @@
     xy_table, xz_table, yz_table = [spread(off, row) for row in range(3)]
     pltpu.make_async_copy(lab, lab, load.at[0]).wait()
     labels = lab[...]
-    e = faces(lookup(kx_table, labels))
+    k = lookup(kx_table, labels)
+    e = faces(k)
     levels, e_in, g, g_end = factor(e, damping)
-    head, tail = labels[0, 0:1].astype(jnp.float32), labels[-1, 7:8].astype(jnp.float32)
-    put_record(mat_x, me_x, [e_in[0:1], g[0:1], g_end[0:1], head, tail])
-    pl.semaphore_wait(barrier, nx - 1 + ny - 1)
-    send_all(mat_x, me_x, nx, "gx", send_x.at[0], recv_x.at[0])
     a, b = lookup(xy_table, labels), lookup(xz_table, labels)
     source = [e - preceding(e)[0], central(a), central(b)]
     pltpu.make_async_copy(pot, pot, load.at[3]).wait()
     solved = [forward(levels, damping * pot[i] + source[i]) for i in range(3)]
-    put_record(box_x, me_x, [s[1][0:1] for s in solved] + [s[2][0:1] for s in solved])
+    pl.semaphore_wait(barrier, nx - 1 + ny - 1)
+    put_record(box_x, me_x, matrix_rows(e_in, g, g_end, k, a, b) + [s[1][0:1] for s in solved] + [s[2][0:1] for s in solved])
     send_all(box_x, me_x, nx, "gx", send_x.at[1], recv_x.at[1])
 
     lanes = labt.shape[0] * 128
@@ -314,34 +314,31 @@
         for t in range(ysteps):
             for c in range(lanes // 128):
                 ft[slot, c, pl.ds(t, 8, stride=ysteps), :] = q[t, :, c * 128 : (c + 1) * 128]
-        natural = get_wide(ft.at[slot])
-        return natural, natural.T[:rows].reshape(steps, 8, cols)
+        return get_wide(ft.at[slot])
 
     put_wide(labt, across(labels))
     ysteps = cols // 8
     labels_y = strided_wide(labt, ysteps)
-    ey = faces(lookup(ky_table, labels_y))
+    ky, ay, by = [lookup(table, labels_y) for table in (ky_table, xy_table, yz_table)]
+    ey = faces(ky)
     levels_y, ey_in, gy, gy_end = factor(ey, damping)
-    head_y, tail_y = labels_y[0, 0:1].astype(jnp.float32), labels_y[-1, 7:8].astype(jnp.float32)
-    put_record(mat_y, me_y, [ey_in[0:1], gy[0:1], gy_end[0:1], head_y, tail_y])
+    put_record(mat_y, me_y, matrix_rows(ey_in, gy, gy_end, ky, ay, by))
     send_all(mat_y, me_y, ny, "gy", send_y.at[0], recv_y.at[0])
-    ay, by = lookup(xy_table, labels_y), lookup(yz_table, labels_y)
     source_y = [central(ay), ey - preceding(ey)[0], central(by)]
     base_y = [forward(levels_y, q) for q in source_y]
     zero = jnp.zeros((1, cols), jnp.float32)
     inner = [backward(levels, kept, zero, zero) for kept, _, _ in solved]
     first_part, last_part = homogeneous(levels)
     first_y_part, last_y_part = homogeneous(levels_y)
-    first_weight, first_share = along(first_y_part, 0)
-    last_weight, last_share = along(last_y_part, 1)
-    first_weight, last_weight = damping * first_weight, damping * last_weight
+    first_share, last_share = along(first_y_part, 0), along(last_y_part, 1)
+    first_out[...], last_out[...] = first_share, last_share
+    first_weight, last_weight = damping * first_share, damping * last_share
 
     wait_all(mat_y, ny, recv_y.at[0])
-    ring_y = ring_factor(mat_y, ny, (ky_table, xy_table, yz_table))
-    wait_all(mat_x, nx, recv_x.at[0])
-    ring_x = ring_factor(mat_x, nx, (kx_table, xy_table, xz_table))
+    ring_y = ring_factor(mat_y, ny)
     wait_all(box_x, nx, recv_x.at[1])
-    ends = ring_solve(box_x, nx, ring_x, (0, 1, 2), me_x, first_x, last_x)
+    ring_x = ring_factor(box_x, nx)
+    ends = ring_solve(box_x.at[pl.ds(9, 6)], nx, ring_x, (0, 1, 2), me_x, first_x, last_x)
     turned = [across(inner[i] + first_part * ends[i][0] + last_part * ends[i][1]) for i in range(3)]
     firsts = [base_y[i][1][0:1] + total((first_weight * turned[i]).reshape(ysteps, 8, lanes)) for i in range(3)]
     lasts = [base_y[i][2][0:1] + total((last_weight * turned[i]).reshape(ysteps, 8, lanes)) for i in range(3)]
@@ -349,29 +346,26 @@
     send_all(box_y, me_y, ny, "gy", send_y.at[1], recv_y.at[1])
 
     row = jnp.zeros((1, lanes), jnp.float32)
-    own = []
     for i in range(3):
         put_wide(ft.at[2 + i], turned[i])
         kept = forward(levels_y, damping * strided_wide(ft.at[2 + i], ysteps) + source_y[i])[0]
-        own.append(along(backward(levels_y, kept, row, row), 2 + i)[1])
+        own_out[i] = along(backward(levels_y, kept, row, row), 2 + i).T[:rows].reshape(steps, 8, cols)
     wait_all(box_y, ny, recv_y.at[1])
     ends = ring_solve(box_y, ny, ring_y, (1, 0, 2), me_y, first_y, last_y)
     for i in range(3):
-        ends_y[2 * i : 2 * i + 1, :] = ends[i][0]
-        ends_y[2 * i + 1 : 2 * i + 2, :] = ends[i][1]
-    column = jnp.concatenate([ends_y[...]] * 16, 0).T[:rows].reshape(steps, 8, 128)
-    for i in range(3):
-        for t in range(steps):
-            out[i, t] = (own[i][t] + first_share[t] * column[t, :, 2 * i : 2 * i + 1]
-                         + last_share[t] * column[t, :, 2 * i + 1 : 2 * i + 2])
-    for box, n, sem in ((mat_x, nx, send_x.at[0]), (box_x, nx, send_x.at[1]), (mat_y, ny, send_y.at[0]), (box_y, ny, send_y.at[1])):
+        ends_out[2 * i : 2 * i + 1, :] = ends[i][0]
+        ends_out[2 * i + 1 : 2 * i + 2, :] = ends[i][1]
+    for box, n, sem in ((box_x, nx, send_x.at[1]), (mat_y, ny, send_y.at[0]), (box_y, ny, send_y.at[1])):
         wait_all(box, n, sem)
 
 
-def store(v, out, sem):
-    steps = v.shape[1]
-    for s in range(8):
-        pltpu.make_async_copy(v.at[:, :, s, :], out.at[:, pl.ds(s * steps, steps), :], sem).start()
+def store(own, first, last, ends, out, v, sem):
+    loads, steps, _, cols = v.shape
+    for i in range(loads):
+        change = first[...] * ends[2 * i : 2 * i + 1, :] + last[...] * ends[2 * i + 1 : 2 * i + 2, :]
+        v[i] = own[i] + change.T[: steps * 8].reshape(steps, 8, cols)
+        for s in range(8):
+            pltpu.make_async_copy(v.at[i, :, s, :], out.at[i, pl.ds(s * steps, steps), :], sem).start()
     pltpu.make_async_copy(v, v, sem).wait()
 
 
@@ -386,21 +380,22 @@
     args = (potential.reshape(loads, rows, cols), labels.reshape(rows, cols), principal, off_diagonal)
     result = pl.pallas_call(
         functools.partial(kernel, nx, ny, damping),
-        out_shape=pltpu.VMEM((loads, steps, 8, cols), jnp.float32),
+        out_shape=[
+            pltpu.VMEM(shape, jnp.float32)
+            for shape in ((loads, steps, 8, cols), (cols, lanes), (cols, lanes), (2 * loads, lanes))
+        ],
         in_specs=[hbm] * 4,
-        out_specs=vmem,
+        out_specs=[vmem] * 4,
         scratch_shapes=[
             pltpu.VMEM((loads, steps, 8, cols), jnp.float32),
             pltpu.VMEM((steps, 8, cols), jnp.int32),
             pltpu.VMEM(principal.shape, jnp.float32),
             pltpu.VMEM(off_diagonal.shape, jnp.float32),
-            pltpu.VMEM((5, nx, cols), jnp.float32),
-            pltpu.VMEM((6, nx, cols), jnp.float32),
-            pltpu.VMEM((5, ny, lanes), jnp.float32),
+            pltpu.VMEM((15, nx, cols), jnp.float32),
+            pltpu.VMEM((9, ny, lanes), jnp.float32),
             pltpu.VMEM((6, ny, lanes), jnp.float32),
             pltpu.VMEM((lanes // 128, cols, 128), jnp.int32),
             pltpu.VMEM((5, lanes // 128, cols, 128), jnp.float32),
-            pltpu.VMEM((8, lanes), jnp.float32),
             pltpu.VMEM((loads * max(nx, 8), cols), jnp.float32),
             pltpu.VMEM((loads * max(nx, 8), cols), jnp.float32),
             pltpu.VMEM((loads * max(ny, 8), lanes), jnp.float32),
@@ -418,11 +413,11 @@
     result = pl.pallas_call(
         store,
         out_shape=pltpu.HBM((loads, rows, cols), jnp.float32),
-        in_specs=[vmem],
+        in_specs=[vmem] * 4,
         out_specs=hbm,
-        scratch_shapes=[pltpu.SemaphoreType.DMA],
+        scratch_shapes=[pltpu.VMEM((loads, steps, 8, cols), jnp.float32), pltpu.SemaphoreType.DMA],
         compiler_params=pltpu.CompilerParams(vmem_limit_bytes=8 * 1024 * 1024),
-    )(pltpu.with_memory_space_constraint(result, pltpu.VMEM))
+    )(*[pltpu.with_memory_space_constraint(x, pltpu.VMEM) for x in result])
     return result.reshape(potential.shape)
 
 

time: 14.5 us -> 13.7 us (0.945)
  Pallas kernels: 14.3 us -> 13.5 us
    pallas_call x1, Pallas kernels: 13.5 us -> 12.7 us  [local(): pl.pallas_call(functools.partial(kernel, nx, ny, damping), out_shape=[plt...]
where the time goes in v3:
time: 13.7 us; the launch traced here: 13.5 us
  Pallas kernels  13.5 us (99%)
    pallas_call x1, Pallas kernels, local(): pl.pallas_call(functools.partial(kernel, nx, ny, damping), out_shape=[plt...  12.7 us
    pallas_call x1, Pallas kernels, local(): pl.pallas_call(store, out_shape=pltpu.HBM((loads, rows, cols), jnp.float3...  0.85 us

profile of v3, /device:TPU:0, one launch (start us, length us, event | category | flops | bytes accessed | tf_op | source)
XLA Modules:
  0.0 13.5 jit_solution(3719039487850047684)
XLA Ops:
  0.0 12.7 %shard_map.46 = (f32[3,32,8,128]{3,2,1,0:T(8,128)S(1)}, f32[128,256]{1,0:T(8,128)S(1)}, f32[128,256]{1,0:T(8,128)S(1)}, f32[6,256]{1,0:T(8,128)S(1)}) custom-call(f32[3,256,128]{2,1,0:T(8,128)} %bitcast.5, s32[256,128]{1,0:T(8,128)} %bitcast.6, f32[2,8]{1,0:T(2,128)} %pri_hbm.1, f32[3,8]{1,0:T(4,128)} %off_hbm.1), custom_call_target="tpu_custom_call" | custom-call | tf_op jit(solution)/shard_map/pallas_call | solution.py:381
  12.7 0.8 %shard_map.47 = f32[3,256,128]{2,1,0:T(8,128)} custom-call(f32[3,32,8,128]{3,2,1,0:T(8,128)S(1)} %get-tuple-element.9.own, f32[128,256]{1,0:T(8,128)S(1)} %get-tuple-element.10.first, f32[128,256]{1,0:T(8,128)S(1)} %get-tuple-element.11.last, f32[6,256]{1,0:T(8,128)S(1)} %get-tuple-element.12.ends), custom_call_target="tpu_custom_call" | custom-call | tf_op jit(solution)/shard_map/pallas_call | solution.py:413

commit v4 on v3

--- a/solution.py
+++ b/solution.py
@@ -65,9 +65,9 @@
 
 def spread(ref, row):
     lane = lax.broadcasted_iota(jnp.int32, (8, 128), 1)
-    out = jnp.broadcast_to(ref[row : row + 1, 0:1], (8, 128))
+    out = jnp.full((8, 128), ref[row, 0], jnp.float32)
     for phase in range(1, 8):
-        out = jnp.where(lane == phase, jnp.broadcast_to(ref[row : row + 1, phase : phase + 1], (8, 128)), out)
+        out = jnp.where(lane == phase, ref[row, phase], out)
     return out
 
 
@@ -84,10 +84,13 @@
     return jnp.stack(out, 0).reshape(labels.shape)
 
 
+def at_end(q, value):
+    end = jnp.where(sublane(q.shape[1:]) == 7, value, q[-1])[None]
+    return end if q.shape[0] == 1 else jnp.concatenate([q[:-1], end], 0)
+
+
 def faces(half_inverse):
-    e = 1.0 / (half_inverse + following(half_inverse, half_inverse[0]))
-    position = lax.broadcasted_iota(jnp.int32, e.shape, 0)
-    return jnp.where((position == e.shape[0] - 1) & (sublane(e.shape) == 7), 0.0, e)
+    return at_end(1.0 / (half_inverse + following(half_inverse, half_inverse[0])), 0.0)
 
 
 def factor(e, damping):
@@ -100,9 +103,8 @@
         g_even, g_odd = split(g)
         r = 1.0 / (e_even + e_odd + g_odd)
         if top:
-            is_end = (lax.broadcasted_iota(jnp.int32, r.shape, 0) == r.shape[0] - 1) & (sublane(r.shape) == 7)
-            r = jnp.where(is_end, 0.0, r)
-            right = jnp.where(is_end, 1.0, e_odd * r)
+            r = at_end(r, 0.0)
+            right = at_end(e_odd * r, 1.0)
         else:
             right = e_odd * r
         left = e_even * r
@@ -132,14 +134,14 @@
     f_end = jnp.zeros(f.shape[1:], jnp.float32)
     for left, right, r in levels[:-3]:
         f_even, f_odd = split(f)
-        kept.append(f_odd * r)
+        kept.append(f_odd)
         moved, wrap = preceding(right * f_odd)
         f = f_even + left * f_odd + moved
         f_end = f_end + wrap
     f = f[0]
     sub = sublane(f.shape)
     for by, (left, right, r) in zip((1, 2, 4), levels[-3:]):
-        kept.append(f * r)
+        kept.append(f)
         wrap = turn(right * f, by)
         f = f + turn(left * f, -by) + jnp.where(sub == 0, 0.0, wrap)
         f_end = f_end + wrap
@@ -147,28 +149,33 @@
 
 
 def backward(levels, kept, first, last):
-    shape = kept[-1].shape
+    shape = levels[-1][2].shape
     sub = sublane(shape)
+    kept = [None] * len(levels) if kept is None else kept
     v = jnp.broadcast_to(first, shape)
     last = jnp.broadcast_to(last, shape)
-    for by, (left, right, r), own in zip((4, 2, 1), levels[:-4:-1], kept[:-4:-1]):
+
+    def between(level, own, low, high):
+        left, right, r = level
+        inner = left * low + right * high
+        return inner if own is None else own * r + inner
+
+    for by, level, own in zip((4, 2, 1), levels[:-4:-1], kept[:-4:-1]):
         after = jnp.where(sub >= 8 - by, last, turn(v, -by))
-        v = jnp.where(sub % (2 * by) == by, own + left * turn(v, by) + right * after, v)
+        v = jnp.where(sub % (2 * by) == by, between(level, own, turn(v, by), after), v)
     v = v[None]
-    for (left, right, r), own in zip(levels[:-3][::-1], kept[:-3][::-1]):
-        odd = own + left * v + right * following(v, last)
-        v = merge(v, odd)
+    for level, own in zip(levels[:-3][::-1], kept[:-3][::-1]):
+        v = merge(v, between(level, own, v, following(v, last)))
     return v
 
 
 def homogeneous(levels):
-    none = [jnp.zeros_like(r) for _, _, r in levels]
     row = jnp.zeros_like(levels[-1][2][0:1])
-    return backward(levels, none, row + 1.0, row), backward(levels, none, row, row + 1.0)
+    return backward(levels, None, row + 1.0, row), backward(levels, None, row, row + 1.0)
 
 
 def central(k):
-    return 0.5 * (following(k, jnp.zeros_like(k[0])) - preceding(k)[0])
+    return following(k, jnp.zeros_like(k[0])) - preceding(k)[0]
 
 
 def matrix_rows(e, g, g_end, k, a, b):
@@ -223,11 +230,13 @@
 
 def ring_factor(box, n):
     e, g, g_end, k_head, k_tail, a_head, a_tail, b_head, b_tail = [get_row(box, n, q) for q in range(9)]
-    link = 1.0 / (k_tail + turn(k_head, -1))
-    gain = [link, 0.5 * turn(a_head, -1), 0.5 * turn(b_head, -1)]
-    loss = [turn(link, 1), turn(0.5 * a_tail, 1), turn(0.5 * b_tail, 1)]
-    r = 1.0 / (e + link + g_end)
-    left, right = e * r, link * r
+    series = k_tail + turn(k_head, -1)
+    link = 1.0 / series
+    gain = [link, turn(a_head, -1), turn(b_head, -1)]
+    loss = [turn(link, 1), turn(a_tail, 1), turn(b_tail, 1)]
+    right = 1.0 / (series * (e + g_end) + 1.0)
+    r = series * right
+    left = e * r
     g = g + left * g_end + turn(right * g_end, 1)
     e = e * right
     levels = []
@@ -259,6 +268,14 @@
     ]
 
 
+def stacked(rows):
+    shape = (8, rows[0].shape[1])
+    out = jnp.zeros(shape, jnp.float32)
+    for i, row in enumerate(rows):
+        out = jnp.where(sublane(shape) == i, row, out)
+    return out
+
+
 def total(x):
     x = jnp.sum(x, axis=0) if x.ndim == 3 else x
     for by in (1, 2, 4):
@@ -271,13 +288,13 @@
     me_x, me_y = lax.axis_index("gx"), lax.axis_index("gy")
     loads, steps, _, cols = pot.shape
     rows = steps * 8
-    for s in range(8):
-        pltpu.make_async_copy(lab_hbm.at[pl.ds(s * steps, steps), :], lab.at[:, s, :], load.at[0]).start()
     small = [pltpu.make_async_copy(src, dst, load.at[i]) for i, (src, dst) in enumerate(((pri_hbm, pri), (off_hbm, off)), 1)]
     for copy in small:
         copy.start()
+    for s in range(8):
+        pltpu.make_async_copy(lab_hbm.at[pl.ds(s * steps, steps), :], lab.at[:, s, :], load.at[0]).start()
     barrier = pltpu.get_barrier_semaphore()
-    for mask in range(1, nx):
+    for mask in range(nx - 1, 0, -1):
         pl.semaphore_signal(barrier, inc=1, device_id={"gx": partner(me_x, mask, nx)}, device_id_type=MESH)
     for mask in range(1, ny):
         pl.semaphore_signal(barrier, inc=1, device_id={"gy": partner(me_y, mask, ny)}, device_id_type=MESH)
@@ -287,19 +304,19 @@
     for copy in small:
         copy.wait()
     kx_table, ky_table = 0.5 / spread(pri, 0), 0.5 / spread(pri, 1)
-    xy_table, xz_table, yz_table = [spread(off, row) for row in range(3)]
+    xy_table, xz_table, yz_table = [0.5 * spread(off, row) for row in range(3)]
     pltpu.make_async_copy(lab, lab, load.at[0]).wait()
     labels = lab[...]
     k = lookup(kx_table, labels)
     e = faces(k)
+    pltpu.make_async_copy(pot, pot, load.at[3]).wait()
     levels, e_in, g, g_end = factor(e, damping)
     a, b = lookup(xy_table, labels), lookup(xz_table, labels)
     source = [e - preceding(e)[0], central(a), central(b)]
-    pltpu.make_async_copy(pot, pot, load.at[3]).wait()
     solved = [forward(levels, damping * pot[i] + source[i]) for i in range(3)]
+    put_record(box_x, me_x, matrix_rows(e_in, g, g_end, k, a, b) + [s[1][0:1] for s in solved] + [s[2][0:1] for s in solved])
     pl.semaphore_wait(barrier, nx - 1 + ny - 1)
-    put_record(box_x, me_x, matrix_rows(e_in, g, g_end, k, a, b) + [s[1][0:1] for s in solved] + [s[2][0:1] for s in solved])
-    send_all(box_x, me_x, nx, "gx", send_x.at[1], recv_x.at[1])
+    send_all(box_x, me_x, nx, "gx", send_x.at[0], recv_x.at[0])
 
     lanes = labt.shape[0] * 128
     repeat = lanes // rows
@@ -333,21 +350,32 @@
     first_share, last_share = along(first_y_part, 0), along(last_y_part, 1)
     first_out[...], last_out[...] = first_share, last_share
     first_weight, last_weight = damping * first_share, damping * last_share
+    turned = [across(q) for q in inner]
+    base_firsts = [base_y[i][1][0:1] + total((first_weight * turned[i]).reshape(ysteps, 8, lanes)) for i in range(3)]
+    base_lasts = [base_y[i][2][0:1] + total((last_weight * turned[i]).reshape(ysteps, 8, lanes)) for i in range(3)]
+    parts = [across(first_part), across(last_part)]
+    response = jnp.concatenate([jnp.concatenate([w * q for w in (first_weight, last_weight)], 1) for q in parts], 0)
+    response_hi = response.astype(jnp.bfloat16)
+    response_lo = (response - response_hi.astype(jnp.float32)).astype(jnp.bfloat16)
 
     wait_all(mat_y, ny, recv_y.at[0])
     ring_y = ring_factor(mat_y, ny)
-    wait_all(box_x, nx, recv_x.at[1])
+    wait_all(box_x, nx, recv_x.at[0])
     ring_x = ring_factor(box_x, nx)
     ends = ring_solve(box_x.at[pl.ds(9, 6)], nx, ring_x, (0, 1, 2), me_x, first_x, last_x)
-    turned = [across(inner[i] + first_part * ends[i][0] + last_part * ends[i][1]) for i in range(3)]
-    firsts = [base_y[i][1][0:1] + total((first_weight * turned[i]).reshape(ysteps, 8, lanes)) for i in range(3)]
-    lasts = [base_y[i][2][0:1] + total((last_weight * turned[i]).reshape(ysteps, 8, lanes)) for i in range(3)]
+    vector = jnp.concatenate([stacked([ends[i][0] for i in range(3)]), stacked([ends[i][1] for i in range(3)])], 1)
+    coarse = vector.astype(jnp.bfloat16).astype(jnp.float32)
+    operand = jnp.concatenate([coarse, vector - coarse], 0).astype(jnp.bfloat16)
+    response = jnp.dot(operand, response_hi, preferred_element_type=jnp.float32)
+    response = response[:8] + response[8:] + jnp.dot(operand, response_lo, preferred_element_type=jnp.float32)[:8]
+    firsts = [base_firsts[i] + response[i : i + 1, :lanes] for i in range(3)]
+    lasts = [base_lasts[i] + response[i : i + 1, lanes:] for i in range(3)]
     put_record(box_y, me_y, firsts + lasts)
     send_all(box_y, me_y, ny, "gy", send_y.at[1], recv_y.at[1])
 
     row = jnp.zeros((1, lanes), jnp.float32)
     for i in range(3):
-        put_wide(ft.at[2 + i], turned[i])
+        put_wide(ft.at[2 + i], turned[i] + across(first_part * ends[i][0] + last_part * ends[i][1]))
         kept = forward(levels_y, damping * strided_wide(ft.at[2 + i], ysteps) + source_y[i])[0]
         own_out[i] = along(backward(levels_y, kept, row, row), 2 + i).T[:rows].reshape(steps, 8, cols)
     wait_all(box_y, ny, recv_y.at[1])
@@ -355,7 +383,7 @@
     for i in range(3):
         ends_out[2 * i : 2 * i + 1, :] = ends[i][0]
         ends_out[2 * i + 1 : 2 * i + 2, :] = ends[i][1]
-    for box, n, sem in ((box_x, nx, send_x.at[1]), (mat_y, ny, send_y.at[0]), (box_y, ny, send_y.at[1])):
+    for box, n, sem in ((box_x, nx, send_x.at[0]), (mat_y, ny, send_y.at[0]), (box_y, ny, send_y.at[1])):
         wait_all(box, n, sem)
 
 
@@ -389,8 +417,8 @@
         scratch_shapes=[
             pltpu.VMEM((loads, steps, 8, cols), jnp.float32),
             pltpu.VMEM((steps, 8, cols), jnp.int32),
-            pltpu.VMEM(principal.shape, jnp.float32),
-            pltpu.VMEM(off_diagonal.shape, jnp.float32),
+            pltpu.SMEM(principal.shape, jnp.float32),
+            pltpu.SMEM(off_diagonal.shape, jnp.float32),
             pltpu.VMEM((15, nx, cols), jnp.float32),
             pltpu.VMEM((9, ny, lanes), jnp.float32),
             pltpu.VMEM((6, ny, lanes), jnp.float32),
@@ -400,8 +428,8 @@
             pltpu.VMEM((loads * max(nx, 8), cols), jnp.float32),
             pltpu.VMEM((loads * max(ny, 8), lanes), jnp.float32),
             pltpu.VMEM((loads * max(ny, 8), lanes), jnp.float32),
-            pltpu.SemaphoreType.DMA((2,)),
-            pltpu.SemaphoreType.DMA((2,)),
+            pltpu.SemaphoreType.DMA((1,)),
+            pltpu.SemaphoreType.DMA((1,)),
             pltpu.SemaphoreType.DMA((2,)),
             pltpu.SemaphoreType.DMA((2,)),
             pltpu.SemaphoreType.DMA((4,)),

time: 13.7 us -> 13.6 us (level)
  no operation moved by 1% of the time
where the time goes in v4:
time: 13.6 us; the launch traced here: 13.4 us
  Pallas kernels  13.4 us (99%)
    pallas_call x1, Pallas kernels, local(): pl.pallas_call(functools.partial(kernel, nx, ny, damping), out_shape=[plt...  12.6 us
    pallas_call x1, Pallas kernels, local(): pl.pallas_call(store, out_shape=pltpu.HBM((loads, rows, cols), jnp.float3...  0.85 us

profile of v4, /device:TPU:0, one launch (start us, length us, event | category | flops | bytes accessed | tf_op | source)
XLA Modules:
  0.0 13.4 jit_solution(12541572940413654164)
XLA Ops:
  0.0 12.6 %shard_map.46 = (f32[3,32,8,128]{3,2,1,0:T(8,128)S(1)}, f32[128,256]{1,0:T(8,128)S(1)}, f32[128,256]{1,0:T(8,128)S(1)}, f32[6,256]{1,0:T(8,128)S(1)}) custom-call(f32[3,256,128]{2,1,0:T(8,128)} %bitcast.5, s32[256,128]{1,0:T(8,128)} %bitcast.6, f32[2,8]{1,0:T(2,128)} %pri_hbm.1, f32[3,8]{1,0:T(4,128)} %off_hbm.1), custom_call_target="tpu_custom_call" | custom-call | tf_op jit(solution)/shard_map/pallas_call | solution.py:409
  12.6 0.8 %shard_map.47 = f32[3,256,128]{2,1,0:T(8,128)} custom-call(f32[3,32,8,128]{3,2,1,0:T(8,128)S(1)} %get-tuple-element.9.own, f32[128,256]{1,0:T(8,128)S(1)} %get-tuple-element.10.first, f32[128,256]{1,0:T(8,128)S(1)} %get-tuple-element.11.last, f32[6,256]{1,0:T(8,128)S(1)} %get-tuple-element.12.ends), custom_call_target="tpu_custom_call" | custom-call | tf_op jit(solution)/shard_map/pallas_call | solution.py:441

commit v5 on v4

--- a/solution.py
+++ b/solution.py
@@ -199,9 +199,9 @@
     return out
 
 
-def send_all(box, me, n, axis, send, recv):
+def send_all(box, me, n, axis, send, recv, begin=0, end=None):
     slot = box.at[:, pl.ds(me, 1), :]
-    for k in range(n - 1):
+    for k in range(begin, n - 1 if end is None else end):
         pltpu.make_async_remote_copy(
             src_ref=slot,
             dst_ref=slot,
@@ -316,7 +316,7 @@
     solved = [forward(levels, damping * pot[i] + source[i]) for i in range(3)]
     put_record(box_x, me_x, matrix_rows(e_in, g, g_end, k, a, b) + [s[1][0:1] for s in solved] + [s[2][0:1] for s in solved])
     pl.semaphore_wait(barrier, nx - 1 + ny - 1)
-    send_all(box_x, me_x, nx, "gx", send_x.at[0], recv_x.at[0])
+    send_all(box_x, me_x, nx, "gx", send_x.at[0], recv_x.at[0], 0, 4)
 
     lanes = labt.shape[0] * 128
     repeat = lanes // rows
@@ -340,6 +340,7 @@
     ey = faces(ky)
     levels_y, ey_in, gy, gy_end = factor(ey, damping)
     put_record(mat_y, me_y, matrix_rows(ey_in, gy, gy_end, ky, ay, by))
+    send_all(box_x, me_x, nx, "gx", send_x.at[0], recv_x.at[0], 4)
     send_all(mat_y, me_y, ny, "gy", send_y.at[0], recv_y.at[0])
     source_y = [central(ay), ey - preceding(ey)[0], central(by)]
     base_y = [forward(levels_y, q) for q in source_y]

time: 13.6 us -> 13.6 us (level)
  no operation moved by 1% of the time
where the time goes in v5:
time: 13.6 us; the launch traced here: 13.4 us
  Pallas kernels  13.4 us (99%)
    pallas_call x1, Pallas kernels, local(): pl.pallas_call(functools.partial(kernel, nx, ny, damping), out_shape=[plt...  12.5 us
    pallas_call x1, Pallas kernels, local(): pl.pallas_call(store, out_shape=pltpu.HBM((loads, rows, cols), jnp.float3...  0.85 us

profile of v5, /device:TPU:0, one launch (start us, length us, event | category | flops | bytes accessed | tf_op | source)
XLA Modules:
  0.0 13.4 jit_solution(2289052674139598651)
XLA Ops:
  0.0 12.5 %shard_map.46 = (f32[3,32,8,128]{3,2,1,0:T(8,128)S(1)}, f32[128,256]{1,0:T(8,128)S(1)}, f32[128,256]{1,0:T(8,128)S(1)}, f32[6,256]{1,0:T(8,128)S(1)}) custom-call(f32[3,256,128]{2,1,0:T(8,128)} %bitcast.5, s32[256,128]{1,0:T(8,128)} %bitcast.6, f32[2,8]{1,0:T(2,128)} %pri_hbm.1, f32[3,8]{1,0:T(4,128)} %off_hbm.1), custom_call_target="tpu_custom_call" | custom-call | tf_op jit(solution)/shard_map/pallas_call | solution.py:410
  12.5 0.8 %shard_map.47 = f32[3,256,128]{2,1,0:T(8,128)} custom-call(f32[3,32,8,128]{3,2,1,0:T(8,128)S(1)} %get-tuple-element.9.own, f32[128,256]{1,0:T(8,128)S(1)} %get-tuple-element.10.first, f32[128,256]{1,0:T(8,128)S(1)} %get-tuple-element.11.last, f32[6,256]{1,0:T(8,128)S(1)} %get-tuple-element.12.ends), custom_call_target="tpu_custom_call" | custom-call | tf_op jit(solution)/shard_map/pallas_call | solution.py:442

commit v6 on v5

--- a/solution.py
+++ b/solution.py
@@ -200,7 +200,7 @@
 
 
 def send_all(box, me, n, axis, send, recv, begin=0, end=None):
-    slot = box.at[:, pl.ds(me, 1), :]
+    slot = box.at[:, pl.ds(place(me, n), 1), :]
     for k in range(begin, n - 1 if end is None else end):
         pltpu.make_async_remote_copy(
             src_ref=slot,
@@ -228,26 +228,42 @@
     return out
 
 
+def place(me, n):
+    return me if n < 16 else lax.rem(me, 2) * (n // 2) + lax.div(me, 2)
+
+
+def circle(x, by):
+    size = x.shape[0]
+    if size < 16:
+        return turn(x, by)
+    low, high = x[: size // 2], x[size // 2 :]
+    if by % 2 == 0:
+        return jnp.concatenate([turn(low, by // 2), turn(high, by // 2)], 0)
+    if by == 1:
+        return jnp.concatenate([turn(high, 1), low], 0)
+    return jnp.concatenate([high, turn(low, -1)], 0)
+
+
 def ring_factor(box, n):
     e, g, g_end, k_head, k_tail, a_head, a_tail, b_head, b_tail = [get_row(box, n, q) for q in range(9)]
-    series = k_tail + turn(k_head, -1)
+    series = k_tail + circle(k_head, -1)
     link = 1.0 / series
-    gain = [link, turn(a_head, -1), turn(b_head, -1)]
-    loss = [turn(link, 1), turn(a_tail, 1), turn(b_tail, 1)]
+    gain = [link, circle(a_head, -1), circle(b_head, -1)]
+    loss = [circle(link, 1), circle(a_tail, 1), circle(b_tail, 1)]
     right = 1.0 / (series * (e + g_end) + 1.0)
     r = series * right
     left = e * r
-    g = g + left * g_end + turn(right * g_end, 1)
+    g = g + left * g_end + circle(right * g_end, 1)
     e = e * right
     levels = []
     by = 1
     while by < n:
-        e_left = turn(e, by)
+        e_left = circle(e, by)
         s = 1.0 / (e_left + e + g)
         lo, hi = e_left * s, e * s
         levels.append((by, lo, hi))
-        g = g + turn(lo * g, -by) + turn(hi * g, by)
-        e = e * turn(hi, -by)
+        g = g + circle(lo * g, -by) + circle(hi * g, by)
+        e = e * circle(hi, -by)
         by *= 2
     return gain, loss, r, left, right, levels, 1.0 / g
 
@@ -257,12 +273,12 @@
     size = inv.shape[0]
     for i, which in enumerate(order):
         end = get_row(box, n, 3 + i) + gain[which]
-        v = get_row(box, n, i) - loss[which] + left * end + turn(right * end, 1)
+        v = get_row(box, n, i) - loss[which] + left * end + circle(right * end, 1)
         for by, lo, hi in levels:
-            v = v + turn(lo * v, -by) + turn(hi * v, by)
+            v = v + circle(lo * v, -by) + circle(hi * v, by)
         v = v * inv
         first_out[i * size : (i + 1) * size, :] = v
-        last_out[i * size : (i + 1) * size, :] = r * end + left * v + right * turn(v, -1)
+        last_out[i * size : (i + 1) * size, :] = r * end + left * v + right * circle(v, -1)
     return [
         (first_out[pl.ds(i * size + me, 1), :], last_out[pl.ds(i * size + me, 1), :]) for i in range(3)
     ]
@@ -314,7 +330,7 @@
     a, b = lookup(xy_table, labels), lookup(xz_table, labels)
     source = [e - preceding(e)[0], central(a), central(b)]
     solved = [forward(levels, damping * pot[i] + source[i]) for i in range(3)]
-    put_record(box_x, me_x, matrix_rows(e_in, g, g_end, k, a, b) + [s[1][0:1] for s in solved] + [s[2][0:1] for s in solved])
+    put_record(box_x, place(me_x, nx), matrix_rows(e_in, g, g_end, k, a, b) + [s[1][0:1] for s in solved] + [s[2][0:1] for s in solved])
     pl.semaphore_wait(barrier, nx - 1 + ny - 1)
     send_all(box_x, me_x, nx, "gx", send_x.at[0], recv_x.at[0], 0, 4)
 
@@ -363,7 +379,7 @@
     ring_y = ring_factor(mat_y, ny)
     wait_all(box_x, nx, recv_x.at[0])
     ring_x = ring_factor(box_x, nx)
-    ends = ring_solve(box_x.at[pl.ds(9, 6)], nx, ring_x, (0, 1, 2), me_x, first_x, last_x)
+    ends = ring_solve(box_x.at[pl.ds(9, 6)], nx, ring_x, (0, 1, 2), place(me_x, nx), first_x, last_x)
     vector = jnp.concatenate([stacked([ends[i][0] for i in range(3)]), stacked([ends[i][1] for i in range(3)])], 1)
     coarse = vector.astype(jnp.bfloat16).astype(jnp.float32)
     operand = jnp.concatenate([coarse, vector - coarse], 0).astype(jnp.bfloat16)

time: 13.6 us -> 13.6 us (level)
  no operation moved by 1% of the time
where the time goes in v6:
time: 13.6 us; the launch traced here: 13.4 us
  Pallas kernels  13.4 us (99%)
    pallas_call x1, Pallas kernels, local(): pl.pallas_call(functools.partial(kernel, nx, ny, damping), out_shape=[plt...  12.5 us
    pallas_call x1, Pallas kernels, local(): pl.pallas_call(store, out_shape=pltpu.HBM((loads, rows, cols), jnp.float3...  0.85 us

profile of v6, /device:TPU:0, one launch (start us, length us, event | category | flops | bytes accessed | tf_op | source)
XLA Modules:
  0.0 13.4 jit_solution(9280062411834004710)
XLA Ops:
  0.0 12.5 %shard_map.46 = (f32[3,32,8,128]{3,2,1,0:T(8,128)S(1)}, f32[128,256]{1,0:T(8,128)S(1)}, f32[128,256]{1,0:T(8,128)S(1)}, f32[6,256]{1,0:T(8,128)S(1)}) custom-call(f32[3,256,128]{2,1,0:T(8,128)} %bitcast.5, s32[256,128]{1,0:T(8,128)} %bitcast.6, f32[2,8]{1,0:T(2,128)} %pri_hbm.1, f32[3,8]{1,0:T(4,128)} %off_hbm.1), custom_call_target="tpu_custom_call" | custom-call | tf_op jit(solution)/shard_map/pallas_call | solution.py:426
  12.5 0.8 %shard_map.47 = f32[3,256,128]{2,1,0:T(8,128)} custom-call(f32[3,32,8,128]{3,2,1,0:T(8,128)S(1)} %get-tuple-element.9.own, f32[128,256]{1,0:T(8,128)S(1)} %get-tuple-element.10.first, f32[128,256]{1,0:T(8,128)S(1)} %get-tuple-element.11.last, f32[6,256]{1,0:T(8,128)S(1)} %get-tuple-element.12.ends), custom_call_target="tpu_custom_call" | custom-call | tf_op jit(solution)/shard_map/pallas_call | solution.py:458
